TPU v7x, 32 devices: a whole 2x2x4 slice. The times are simulated.
32 devices in a mesh: group: 2 (over y), seq: 8 (over z, core), mp: 2 (over x).
Axes of the slice: x: 2, y: 2, z: 4, core: 2. Of those that a mesh axis runs over, the one named last changes fastest.
Arguments:
- hidden: bfloat16 [2, 4096, 4096], P('group', 'seq', 'mp'), may hold values from -16 to 16
- w_qkv: bfloat16 [8, 4096, 768], P('mp'), may hold values from -0.09375 to 0.09375
- cache: bfloat16 [1024, 128, 8, 256], P('seq', None, 'mp'), may hold values from -16 to 16
- cache_len: int32 [1024], P('seq'), may hold values from 1 to 128, as said below
- receive: int32 [1024], P('seq'), may hold values 0 or 1
Outputs:
- attended: bfloat16 [2, 4096, 4096], P('group', 'seq', 'mp')
Inputs may be any that keep to these rules, and one draw needn't show every extreme that they name: `cache_len`: in each seq shard's 128 requests one has length 128.
All inputs are finite; a program needn't handle non-finite values. No bound on the sum of `receive` on one device may be relied on, other than what follows from the above.
Results may differ from a plain program's by a relative error of at most 0.0098.
Values may be sent and summed in bfloat16 or wider, within the bound.
No kernel may reach another device: no remote copies, remote signals or barrier semaphores. Data moves between devices by JAX's collectives and lax.ppermute only.
A program may use at most 384 MiB of HBM per device.

v0:
```python
import functools

import jax
import jax.numpy as jnp
from jax import lax
from jax.experimental import pallas as pl
from jax.experimental.pallas import tpu as pltpu
from jax.sharding import PartitionSpec as P

MASKED_SCORE = -1e30
SUB_REQ = 8
LANES = 128
CHUNKS = 2
PAD = 16
SAFE_LOGIT = 60.0
LOG2E = 1.4426950408889634
MIB = 1 << 20
NT = (((1,), (1,)), ((), ()))
NN = (((1,), (0,)), ((), ()))
ANY = pl.BlockSpec(memory_space=pltpu.HBM)
SMALL, LARGE = 1000, 200_000_000_000


def passed_along(block, axis, distance):
    devices = range(lax.axis_size(axis))
    route = [(i - distance, i) for i in devices if i - distance in devices]
    return lax.ppermute(block, axis, route)


def dot(a, b, dims):
    return lax.dot_general(a, b, dims, preferred_element_type=jnp.float32)


def call(kernel, name, grid, prefetch, in_specs, out_specs, out_shape, scratch=(), cost=SMALL, mib=48, aliases=None):
    made = pl.pallas_call(
        kernel,
        grid_spec=pltpu.PrefetchScalarGridSpec(
            num_scalar_prefetch=prefetch,
            grid=grid,
            in_specs=in_specs,
            out_specs=out_specs,
            scratch_shapes=list(scratch),
        ),
        out_shape=out_shape,
        input_output_aliases=aliases or {},
        compiler_params=pltpu.CompilerParams(
            dimension_semantics=("arbitrary",) * len(grid), vmem_limit_bytes=mib * MIB
        ),
        cost_estimate=pl.CostEstimate(flops=cost, bytes_accessed=SMALL, transcendentals=0),
        name=name,
    )

    def on(*args):
        kept = [pltpu.with_memory_space_constraint(x, pltpu.HBM) for x in args[prefetch:]]
        return made(*args[:prefetch], *kept)

    return on


def after_all(block, *before):
    return pl.pallas_call(
        lambda *refs: None,
        in_specs=[ANY] * (1 + len(before)),
        out_specs=ANY,
        out_shape=jax.ShapeDtypeStruct(block.shape, block.dtype),
        input_output_aliases={0: 0},
        name="after_all",
    )(block, *before)


def longest_row(x):
    wide = x.astype(jnp.float32)
    return jnp.max(jnp.sum(wide * wide, axis=1, keepdims=True), axis=0, keepdims=True)


def project_kernel(heads, ids, own, own_s, oth, oth_s, w, *refs):
    q_out, theirs, mine_kv, norms, kv0, kv1, total, top_rows = refs[-8:]
    gi, half = pl.program_id(0), pl.program_id(1)
    rows = own.shape[0]

    def product(mine, others):
        return dot(jnp.concatenate([mine[...], others[...]], axis=0), w[0], NN)

    @pl.when(half == 0)
    def _():
        total[...] = product(own, own_s)

    @pl.when(half == 1)
    def _():
        width = w.shape[2] // (heads + 2)
        longest = jnp.zeros((1, 1), jnp.float32)
        both = (total[...] + product(oth, oth_s)).astype(jnp.bfloat16)
        for side in range(2):
            here = slice(side * rows, (side + 1) * rows)
            res = both[here]
            for h in range(heads):
                q = res[:, h * width : (h + 1) * width]
                q_out[0, side, h * rows : (h + 1) * rows, :] = q
                longest = jnp.maximum(longest, longest_row(q))
            if side == 0:
                mine_kv[0] = res[:, heads * width :]
            else:
                theirs[0] = res

            def ring_form(out):
                k = res[:, heads * width : (heads + 1) * width]
                out[here, :width] = k
                for tile in range(rows // width):
                    lo = tile * width
                    out[side * rows + lo : side * rows + lo + width, width:] = res[
                        lo : lo + width, (heads + 1) * width :
                    ].T
                top = jnp.broadcast_to(longest_row(k) * 1.01, (PAD // 2, 2 * width))
                low = 2 * rows + side * (PAD // 2)
                top_rows[low - 2 * rows : low - 2 * rows + PAD // 2] = top

            @pl.when(gi == 0)
            def _():
                ring_form(kv0)

            @pl.when(gi == 1)
            def _():
                ring_form(kv1)

        norms[0] = jnp.broadcast_to(longest, norms.shape[1:])
        bound = top_rows[...].astype(jnp.bfloat16)

        @pl.when(gi == 0)
        def _():
            kv0[2 * rows :] = bound

        @pl.when(gi == 1)
        def _():
            kv1[2 * rows :] = bound


def project(ids, own, own_s, oth, oth_s, w, before, chunk, after, cost):
    rows, width = oth.shape
    columns = w.shape[2]
    kv_cols = columns // 3
    heads = 4
    head_width = kv_cols // 2

    x_specs = [pl.BlockSpec((rows, width), lambda i, half, ids: (chunk, 0))] * 2
    x_specs += [pl.BlockSpec((rows, width), lambda i, half, ids: (0, 0))] * 2
    in_specs = x_specs + [
        pl.BlockSpec((1, width, columns), lambda i, half, ids: (2 * ids[0] + i, half ^ ids[3], 0))
    ]
    args = [ids, own, own_s, oth, oth_s, w]
    aliases = {}
    if before is not None:
        aliases = {len(args): 0}
        in_specs.append(ANY)
        args.append(before)
    ring_shape = (2 * rows + PAD, kv_cols)
    whole = pl.BlockSpec(ring_shape, lambda i, half, ids: (0, 0))
    return call(
        functools.partial(project_kernel, heads),
        "project",
        (2, 2),
        1,
        in_specs + [ANY] * len(after),
        [
            pl.BlockSpec((1, 2, heads * rows, head_width), lambda i, half, ids: (i, chunk, 0, 0)),
            pl.BlockSpec((1, rows, columns), lambda i, half, ids: (i, 0, 0)),
            pl.BlockSpec((1, rows, kv_cols), lambda i, half, ids: (i, 0, 0)),
            pl.BlockSpec((1, 8, LANES), lambda i, half, ids: (i, 0, 0)),
            whole,
            whole,
        ],
        [
            jax.ShapeDtypeStruct((2, 2 * CHUNKS, heads * rows, head_width), jnp.bfloat16),
            jax.ShapeDtypeStruct((2, rows, columns), jnp.bfloat16),
            jax.ShapeDtypeStruct((2, rows, kv_cols), jnp.bfloat16),
            jax.ShapeDtypeStruct((2, 8, LANES), jnp.float32),
            jax.ShapeDtypeStruct(ring_shape, jnp.bfloat16),
            jax.ShapeDtypeStruct(ring_shape, jnp.bfloat16),
        ],
        [
            pltpu.VMEM((2 * rows, columns), jnp.float32),
            pltpu.VMEM((PAD, kv_cols), jnp.float32),
        ],
        cost=cost,
        mib=56,
        aliases=aliases,
    )(*args, *after)


def cache_kernel(side, heads, draft, start_req, first_step, scale, ids, lens, receive, cache, *refs):
    out = refs[-1]
    _, step_req, slots, both = cache.shape
    width = both // 2
    rows = SUB_REQ * draft
    stacked = heads * rows
    step = pl.program_id(0) + first_step
    factor = scale * LOG2E

    @pl.when(ids[2] == 1)
    def _():
        row = lax.broadcasted_iota(jnp.int32, (stacked, slots), 0)
        req_of_row = row % rows // draft
        slot = lax.broadcasted_iota(jnp.int32, (stacked, slots), 1)
        own_row = lax.broadcasted_iota(jnp.int32, (stacked, rows), 0) % rows
        own_key = lax.broadcasted_iota(jnp.int32, (stacked, rows), 1)
        own_bias = jnp.where(
            (own_row // draft == own_key // draft) & (own_key <= own_row), 0.0, MASKED_SCORE
        )
        lane = lax.broadcasted_iota(jnp.int32, (rows, LANES), 1)
        req_of_lane_row = lax.broadcasted_iota(jnp.int32, (rows, LANES), 0) // draft
        chains, biases, flags = [], [], []
        for sub in range(step_req // SUB_REQ):
            req0 = start_req + step * step_req + sub * SUB_REQ
            biases.append(
                jnp.concatenate(
                    [
                        jnp.where((req_of_row == r) & (slot < lens[req0 + r]), 0.0, MASKED_SCORE)
                        for r in range(SUB_REQ)
                    ],
                    axis=1,
                )
            )
            flag = jnp.zeros((rows, LANES), jnp.float32)
            for r in range(SUB_REQ):
                flag = jnp.where(
                    (req_of_lane_row == r) & (receive[req0 + r] > 0) & (lane == heads), 1.0, flag
                )
            flags.append(flag)
            here = slice(sub * rows, (sub + 1) * rows)
            for gi in range(2):
                if side == 0:
                    q = refs[0]
                    per_head = q.shape[2] // heads
                    row0 = pl.multiple_of(step * (step_req * draft) + sub * rows, rows)
                    queries = [q[gi, 0, pl.ds(h * per_head + row0, rows), :] for h in range(heads)]
                    own = refs[1][gi, here, :]
                else:
                    block = refs[0][gi, here, :]
                    queries = [block[:, h * width : (h + 1) * width] for h in range(heads)]
                    own = block[:, heads * width :]
                kv = cache[gi, sub * SUB_REQ : (sub + 1) * SUB_REQ].reshape(SUB_REQ * slots, both)
                chains.append((gi, sub, here, jnp.concatenate(queries, axis=0), own, kv))
        s = [dot(q, kv[:, :width], NT) for _, _, _, q, own, kv in chains]
        s_own = [dot(q, own[:, :width], NT) for _, _, _, q, own, kv in chains]
        s = [x * factor + biases[chain[1]] for x, chain in zip(s, chains)]
        s_own = [x * factor + own_bias for x in s_own]
        top = [
            jnp.maximum(jnp.max(a, axis=1, keepdims=True), jnp.max(b, axis=1, keepdims=True))
            for a, b in zip(s, s_own)
        ]
        p = [jnp.exp2(x - t) for x, t in zip(s, top)]
        p_own = [jnp.exp2(x - t) for x, t in zip(s_own, top)]
        total = [
            jnp.sum(a, axis=1, keepdims=True) + jnp.sum(b, axis=1, keepdims=True)
            for a, b in zip(p, p_own)
        ]
        o = [
            dot(a.astype(jnp.bfloat16), kv[:, width:], NN)
            + dot(b.astype(jnp.bfloat16), own[:, width:], NN)
            for a, b, (_, _, _, _, own, kv) in zip(p, p_own, chains)
        ]
        for i, (gi, sub, here, _, _, _) in enumerate(chains):
            scaled = o[i] / total[i]
            lse = top[i] + jnp.log2(total[i])
            extra = flags[sub]
            for h in range(heads):
                part = slice(h * rows, (h + 1) * rows)
                out[gi, here, h * width : (h + 1) * width] = scaled[part]
                extra = jnp.where(lane == h, lse[part], extra)
            out[gi, here, heads * width :] = extra


def cache_attention(
    side, ids, lens, receive, cache_t, operands, chunk, rows, draft, scale, heads, after, cost, span=None, before=None
):
    _, _, slots, both = cache_t.shape
    width = both // 2
    step_req = 2 * SUB_REQ
    step_rows = step_req * draft
    steps = rows // step_rows
    lo, hi = span or (0, steps)
    first = chunk * steps + lo
    if side == 0:
        specs = [
            pl.BlockSpec(
                (2, 1, heads * rows, width), lambda i, ids, lens, receive: (0, 2 * chunk, 0, 0)
            )
        ]
        specs += [pl.BlockSpec((2, step_rows, both), lambda i, ids, lens, receive: (0, lo + i, 0))]
    else:
        columns = operands[0].shape[2]
        specs = [
            pl.BlockSpec((2, step_rows, columns), lambda i, ids, lens, receive: (0, lo + i, 0))
        ]

    aliases = {}
    if before is not None:
        aliases = {4 + len(operands) + len(after): 0}
        after = [*after, before]

    def cache_map(i, ids, lens, receive):
        return (ids[0] ^ side, (first + i) * ids[2], 0, 0)

    return call(
        functools.partial(cache_kernel, side, heads, draft, chunk * rows // draft, lo, scale),
        "cache_attention",
        (hi - lo,),
        3,
        [pl.BlockSpec((2, step_req, slots, both), cache_map)] + specs + [ANY] * len(after),
        pl.BlockSpec(
            (2, step_rows, heads * width + LANES), lambda i, ids, lens, receive: (0, lo + i, 0)
        ),
        jax.ShapeDtypeStruct((2, rows, heads * width + LANES), jnp.float32),
        cost=cost,
        aliases=aliases,
    )(ids, lens, receive, cache_t, *operands, *after)


def prompt_kernel(heads, slots_n, rows_core, scale, ids, *refs):
    refs = list(refs)
    norms = [refs.pop(0) for _ in range(CHUNKS)]
    q = refs.pop(0)
    own = [[refs.pop(0), refs.pop(0)] for _ in range(CHUNKS)]
    arrived = [[refs.pop(0) for _ in range(slots_n)] for _ in range(CHUNKS)]
    parts = [refs.pop(0) for _ in range(2 * CHUNKS)]
    outs = refs[-10:-8]
    kvbuf, kd, vt, acc, m_ref, part_ref, fast, sems = refs[-8:]
    gi, blk = pl.program_id(0), pl.program_id(1)
    core, z, grp = ids[0], ids[1], ids[2]
    chips = slots_n // 2
    place = jnp.where(grp == 0, z, slots_n - 1 - z)
    keys = kvbuf.shape[3] - PAD
    stacked, width = q.shape[2:]
    rows = stacked // heads

    def each(act):
        for c in range(CHUNKS):
            for t in range(slots_n):
                r = lax.rem(place - t + slots_n, slots_n)
                chip = jnp.where(r < chips, r, slots_n - 1 - r)
                lane = jnp.where(r < chips, 0, 1)
                act(pltpu.make_async_copy(arrived[c][t], kvbuf.at[lane, c, chip], sems.at[c, t]))

    def place_block(c, at, block):
        k = block[:keys, :width]
        kd[c, at * keys : (at + 1) * keys, :width] = k
        kd[c, at * keys : (at + 1) * keys, width:] = k
        for lo in range(0, keys, width):
            vt[c, :width, at * keys + lo : at * keys + lo + width] = block[lo : lo + width, width:]
        return block[keys:, :].astype(jnp.float32)

    @pl.when((gi == 0) & (blk == 0))
    def _():
        each(lambda copy: copy.start())
        row = lax.broadcasted_iota(jnp.int32, (PAD, vt.shape[2]), 0)
        for c in range(CHUNKS):
            vt[c, width:, :] = jnp.where(row == 0, 1.0, 0.0).astype(jnp.bfloat16)
        each(lambda copy: copy.wait())

    @pl.when(blk == 0)
    def _():
        longest = jnp.zeros((PAD, 2 * width), jnp.float32)
        for c in range(CHUNKS):
            for at in range(chips):
                longest = jnp.maximum(longest, place_block(c, at, kvbuf.at[gi, c, at]))
            for g in range(2):

                @pl.when(gi == g)
                def _(c=c, g=g):
                    part_ref[:PAD, : 2 * width] = place_block(c, chips, own[c][g])

            longest = jnp.maximum(longest, part_ref[:PAD, : 2 * width])
        top_q = norms[0][...]
        for other in norms[1:]:
            top_q = jnp.maximum(top_q, other[...])
        fast[0] = jnp.where(
            jnp.max(longest) * jnp.max(top_q) * (1.02 * scale * scale)
            <= SAFE_LOGIT * SAFE_LOGIT,
            1.0,
            0.0,
        )

    acc[...] = jnp.zeros_like(acc)
    m_ref[...] = jnp.where(fast[0] > 0, 0.0, jnp.full_like(m_ref, MASKED_SCORE))

    wide = q[0, 0].astype(jnp.float32) * (scale * LOG2E)
    high = wide.astype(jnp.bfloat16)
    low = (wide - high.astype(jnp.float32)).astype(jnp.bfloat16)
    q2 = jnp.concatenate([high, low], axis=1)

    side = blk % 2
    pos = (core ^ side) * rows_core + blk // 2 * rows
    full_n = jnp.where(grp == 0, z, chips)

    def admitted(key_start):
        shape = (keys, stacked)
        key = lax.broadcasted_iota(jnp.int32, shape, 0)
        key_core = jnp.where(key >= rows, 1 - core, core)
        key_pos = key_start + key_core * rows_core + jnp.where(key >= rows, key - rows, key)
        row_pos = pos + lax.broadcasted_iota(jnp.int32, shape, 1) % rows
        return key_pos <= row_pos

    def scores(c, at, n):
        return dot(kd[c, pl.ds(at, n * keys)], q2, NT)

    def weighted(c, at, n, p):
        return dot(vt[c, :, pl.ds(at, n * keys)], p.astype(jnp.bfloat16), NN)

    def own_on(c):
        return (grp == 0) & (c * rows <= pos + rows - 1)

    @pl.when(fast[0] > 0)
    def _():
        for n in range(1, chips + 1):

            @pl.when(full_n == n)
            def _(n=n):
                for c in range(CHUNKS):
                    acc[...] = acc[...] + weighted(c, 0, n, jnp.exp2(scores(c, 0, n)))

        for c in range(CHUNKS):

            @pl.when(own_on(c))
            def _(c=c):
                p = jnp.where(admitted(c * rows), jnp.exp2(scores(c, chips * keys, 1)), 0.0)
                acc[...] = acc[...] + weighted(c, chips * keys, 1, p)

    @pl.when(fast[0] == 0)
    def _():
        def visit(c, at, s):
            old = m_ref[:1]
            new = jnp.maximum(old, jnp.max(s, axis=0, keepdims=True))
            acc[...] = acc[...] * jnp.exp2(old - new) + weighted(c, at, 1, jnp.exp2(s - new))
            m_ref[...] = jnp.broadcast_to(new, m_ref.shape)

        for c in range(CHUNKS):

            def body(chip, carry, c=c):
                at = pl.multiple_of(chip * keys, keys)
                visit(c, at, scores(c, at, 1))
                return carry

            lax.fori_loop(0, full_n, body, 0)

            @pl.when(own_on(c))
            def _(c=c):
                s = scores(c, chips * keys, 1)
                visit(c, chips * keys, jnp.where(admitted(c * rows), s, MASKED_SCORE))

    total = acc[width : width + 1]

    def write(merged):
        for h in range(heads):
            columns = slice(h * width, (h + 1) * width)
            value = merged[h * rows : (h + 1) * rows].astype(jnp.bfloat16)
            for sd in range(2):

                @pl.when(side == sd)
                def _(sd=sd, columns=columns, value=value):
                    outs[sd][:, columns] = value

    @pl.when(grp == 0)
    def _():
        write((acc[:width] * (1.0 / total)).T)

    @pl.when(grp == 1)
    def _():
        for i in range(2 * CHUNKS):

            @pl.when(blk == i)
            def _(i=i):
                part_ref[...] = parts[i][0]

        extra = part_ref[:, heads * width :].T
        lse_c = jnp.concatenate([extra[h : h + 1] for h in range(heads)], axis=1)
        flag = jnp.concatenate([extra[heads : heads + 1]] * heads, axis=1)
        o_c = jnp.concatenate(
            [part_ref[:, h * width : (h + 1) * width].T for h in range(heads)], axis=1
        )
        lse_p = jnp.where(flag > 0, m_ref[:1] + jnp.log2(total), MASKED_SCORE)
        top = jnp.maximum(lse_p, lse_c)
        w_p = jnp.exp2(lse_p - top)
        w_c = jnp.exp2(lse_c - top)
        rest = 1.0 / (w_p + w_c)
        write((acc[:width] * (w_p * rest / total) + o_c * (w_c * rest)).T)


def prompt_attention(heads, ids, norms, q, own, arrived, parts, rows_core, scale, after):
    slots_n = len(arrived[0])
    _, blocks, stacked, width = q.shape
    rows = stacked // heads
    keys = 2 * rows
    chips = slots_n // 2
    part_shape = (rows, heads * width + LANES)
    in_specs = [pl.BlockSpec(n.shape, lambda gi, blk, ids: (0, 0, 0)) for n in norms]
    in_specs += [pl.BlockSpec((1, 1, stacked, width), lambda gi, blk, ids: (gi, blk, 0, 0))]
    in_specs += [pl.BlockSpec((keys + PAD, 2 * width), lambda gi, blk, ids: (0, 0))] * (2 * CHUNKS)
    in_specs += [ANY] * (slots_n * CHUNKS)
    in_specs += [pl.BlockSpec((1,) + part_shape, lambda gi, blk, ids: (gi, 0, 0))] * len(parts)
    in_specs += [ANY] * len(after)
    out_block = (rows, heads * width)
    return call(
        functools.partial(prompt_kernel, heads, slots_n, rows_core, scale),
        "prompt_attention",
        (2, blocks),
        1,
        in_specs,
        [
            pl.BlockSpec(out_block, lambda gi, blk, ids: (blk // 2, 2 * ids[0] + gi)),
            pl.BlockSpec(out_block, lambda gi, blk, ids: (blk // 2, gi)),
        ],
        [
            jax.ShapeDtypeStruct((rows_core, 4 * heads * width), jnp.bfloat16),
            jax.ShapeDtypeStruct((rows_core, 2 * heads * width), jnp.bfloat16),
        ],
        [
            pltpu.VMEM((2, CHUNKS, chips, keys + PAD, 2 * width), jnp.bfloat16),
            pltpu.VMEM((CHUNKS, (chips + 1) * keys, 2 * width), jnp.bfloat16),
            pltpu.VMEM((CHUNKS, width + PAD, (chips + 1) * keys), jnp.bfloat16),
            pltpu.VMEM((width + PAD, stacked), jnp.float32),
            pltpu.VMEM((8, stacked), jnp.float32),
            pltpu.VMEM(part_shape, jnp.float32),
            pltpu.SMEM((1,), jnp.float32),
            pltpu.SemaphoreType.DMA((CHUNKS, slots_n)),
        ],
        cost=LARGE,
        mib=58,
    )(ids, *norms, q, *own[0], *own[1], *arrived[0], *arrived[1], *parts, *after)


def fill_kernel(ids, out_before, back, out):
    out[...] = back[...]


def fill_other_half(ids, out, back):
    rows, half = back.shape
    block = (rows // 2, half)
    return call(
        fill_kernel,
        "fill_other_half",
        (2,),
        1,
        [ANY, pl.BlockSpec(block, lambda i, ids: (i, 0))],
        pl.BlockSpec(block, lambda i, ids: (i, 1 - ids[0])),
        jax.ShapeDtypeStruct(out.shape, out.dtype),
        aliases={1: 0},
    )(ids, out, back)


def fast_shards(hidden, w_qkv, cache, cache_len, receive):
    head_width = cache.shape[3] // 2
    heads = w_qkv.shape[2] // head_width - 2
    rows_core = hidden.shape[1]
    rows = rows_core // CHUNKS
    draft = rows_core // cache.shape[0]
    scale = head_width ** (-0.5)
    seq_n = lax.axis_size("seq")
    chips = seq_n // 2
    ring_n = 2 * chips

    seq_i, group_i, mp_i = lax.axis_index("seq"), lax.axis_index("group"), lax.axis_index("mp")
    core = seq_i % 2
    ids = jnp.stack([core, seq_i // 2, group_i, mp_i]).astype(jnp.int32)

    mp_swap = [(0, 1), (1, 0)]
    core_swap = [(i, i ^ 1) for i in range(seq_n)]
    ring = [(0, k) for k in range(chips)] + [(1, chips - 1 - k) for k in range(chips)]
    index = [[g * seq_n + 2 * k + c for c in range(2)] for g, k in ring]
    up = [(index[r][c], index[(r + 1) % ring_n][c]) for r in range(ring_n) for c in range(2)]
    down = [(index[r][c], index[r - 1][c]) for r in range(ring_n) for c in range(2)]

    def swap_cores(x):
        return lax.ppermute(x, "seq", core_swap)

    def round_the_ring(block):
        ups, downs = [block], [block]
        for step in range(ring_n // 2):
            ups.append(lax.ppermute(ups[-1], ("group", "seq"), up))
            if step < ring_n // 2 - 1:
                downs.append(lax.ppermute(downs[-1], ("group", "seq"), down))
        return ups + downs[:0:-1]

    prefill = group_i == 0
    own = hidden[0]
    oth = [lax.ppermute(own[c * rows : (c + 1) * rows], "mp", mp_swap) for c in range(CHUNKS)]
    own_s = swap_cores(own)
    cache_t = jnp.transpose(cache, (2, 0, 1, 3))

    def cached(side, chunk, operands, after, span=None, before=None):
        common = (ids, cache_len, receive, cache_t, operands, chunk, rows, draft, scale, heads)
        return cache_attention(side, *common, after, LARGE, span, before)

    def projected(chunk, before, cost):
        return project(ids, own, own_s, oth[chunk], swap_cores(oth[chunk]), w_qkv, before, chunk, [], cost)

    oth[0] = after_all(oth[0], cache_t)
    q, theirs_0, kv_0, norms_0, kv0_0, kv1_0 = projected(0, None, SMALL)
    crossed_0 = lax.ppermute(kv1_0, "group", [(0, 1)])
    swapped_0 = swap_cores(theirs_0)
    oth[1] = after_all(oth[1], kv_0)

    q, theirs_1, kv_1, norms_1, kv0_1, kv1_1 = projected(1, q, LARGE)
    crossed_1 = lax.ppermute(kv1_1, "group", [(0, 1)])
    swapped_1 = swap_cores(theirs_1)
    ring_0 = round_the_ring(jnp.where(prefill, kv0_0, after_all(crossed_0, kv_1)))
    near_0 = cached(0, 0, (q, kv_0), [])
    ring_1 = round_the_ring(jnp.where(prefill, kv0_1, crossed_1))
    far_0 = cached(1, 0, (swapped_0,), [near_0])
    away_0 = swap_cores(far_0)
    far_1 = cached(1, 1, (swapped_1,), [far_0])
    away_1 = swap_cores(far_1)
    near_1 = cached(0, 1, (q, kv_1), [far_1])

    mine, theirs = prompt_attention(
        heads,
        ids,
        [norms_0, norms_1],
        q,
        [(kv0_0, kv1_0), (kv0_1, kv1_1)],
        [ring_0, ring_1],
        [near_0, away_0, near_1, away_1],
        rows_core,
        scale,
        [],
    )
    return fill_other_half(ids, mine, swap_cores(theirs))[None]


def plain_shards(hidden, w_qkv, cache, cache_len, receive):
    group_count = w_qkv.shape[0]
    column_count = w_qkv.shape[2]
    head_width = cache.shape[3] // 2
    heads_per_group = column_count // head_width - 2
    row_count = hidden.shape[1]
    requests = cache.shape[0]
    draft_count = row_count // requests
    slot_count = cache.shape[1]
    score_scale = head_width ** (-0.5)
    projected = jnp.einsum(
        "rd,gdc->grc",
        lax.all_gather(hidden, "mp", axis=2, tiled=True)[0],
        w_qkv,
        preferred_element_type=jnp.float32,
    ).astype(jnp.bfloat16)
    queries = projected[:, :, : heads_per_group * head_width].reshape(
        group_count, row_count, heads_per_group, head_width
    )
    new_kv = projected[:, :, heads_per_group * head_width :]
    prefill = lax.axis_index("group") == 0
    decode_on = jnp.logical_not(prefill)
    query_pos = lax.axis_index("seq") * row_count + jnp.arange(row_count, dtype=jnp.int32)
    admitted = jnp.repeat(receive, draft_count) > 0
    query_req = queries.reshape(group_count, requests, draft_count, heads_per_group, head_width)
    own_keys = new_kv[..., :head_width].reshape(group_count, requests, draft_count, head_width)
    own_values = new_kv[..., head_width:].reshape(group_count, requests, draft_count, head_width)
    cache_logits = (
        jnp.einsum(
            "gbtph,bugh->gbtpu",
            query_req,
            cache[..., :head_width],
            preferred_element_type=jnp.float32,
        )
        * score_scale
    )
    own_logits = (
        jnp.einsum("gbtph,gbuh->gbtpu", query_req, own_keys, preferred_element_type=jnp.float32)
        * score_scale
    )
    live_cache = (
        (jnp.arange(slot_count, dtype=jnp.int32)[None, :] < cache_len[:, None]) & decode_on
    )[None, :, None, None, :]
    causal = jnp.arange(draft_count)[None, :] <= jnp.arange(draft_count)[:, None]
    live_own = (causal & decode_on)[None, None, :, None, :]
    running_max = jnp.maximum(
        jnp.max(jnp.where(live_cache, cache_logits, MASKED_SCORE), axis=-1),
        jnp.max(jnp.where(live_own, own_logits, MASKED_SCORE), axis=-1),
    )
    cache_weights = jnp.where(live_cache, jnp.exp(cache_logits - running_max[..., None]), 0.0)
    own_weights = jnp.where(live_own, jnp.exp(own_logits - running_max[..., None]), 0.0)
    running_sum = jnp.sum(cache_weights, axis=-1) + jnp.sum(own_weights, axis=-1)
    weighted = jnp.einsum(
        "gbtpu,bugh->gbtph",
        cache_weights.astype(jnp.bfloat16),
        cache[..., head_width:],
        preferred_element_type=jnp.float32,
    )
    weighted = weighted + jnp.einsum(
        "gbtpu,gbuh->gbtph",
        own_weights.astype(jnp.bfloat16),
        own_values,
        preferred_element_type=jnp.float32,
    )
    carried_state = (
        running_max.reshape(group_count, row_count, heads_per_group),
        running_sum.reshape(group_count, row_count, heads_per_group),
        weighted.reshape(group_count, row_count, heads_per_group, head_width),
    )
    assembled = lax.all_gather(new_kv, "seq", axis=1, tiled=True)
    arrived = passed_along(assembled, "group", 1)
    prompt_kv = jnp.where(prefill, assembled, arrived)
    old_max, old_sum, old_weighted = carried_state
    key_count = prompt_kv.shape[1]
    logits = (
        jnp.einsum(
            "grph,gjh->grpj",
            queries,
            prompt_kv[..., :head_width],
            preferred_element_type=jnp.float32,
        )
        * score_scale
    )
    key_pos = jnp.arange(key_count, dtype=jnp.int32)
    allowed = jnp.where(prefill, key_pos[None, :] <= query_pos[:, None], admitted[:, None])[
        None, :, None, :
    ]
    new_max = jnp.maximum(old_max, jnp.max(jnp.where(allowed, logits, MASKED_SCORE), axis=-1))
    weights = jnp.where(allowed, jnp.exp(logits - new_max[..., None]), 0.0)
    rescale = jnp.exp(old_max - new_max)
    new_sum = old_sum * rescale + jnp.sum(weights, axis=-1)
    new_weighted = old_weighted * rescale[..., None] + jnp.einsum(
        "grpj,gjh->grph",
        weights.astype(jnp.bfloat16),
        prompt_kv[..., head_width:],
        preferred_element_type=jnp.float32,
    )
    carried_state = (new_max, new_sum, new_weighted)
    final_max, final_sum, final_weighted = carried_state
    output = (final_weighted / final_sum[..., None]).astype(jnp.bfloat16)
    return jnp.transpose(output, (1, 0, 2, 3)).reshape(
        1, row_count, group_count * heads_per_group * head_width
    )


def solution(mesh):
    def shards(hidden, w_qkv, cache, cache_len, receive):
        head_width = cache.shape[3] // 2
        fits = (
            mesh.shape["group"] == 2
            and mesh.shape["mp"] == 2
            and mesh.shape["seq"] % 2 == 0
            and w_qkv.shape[0] == 4
            and w_qkv.shape[2] == 6 * head_width
            and head_width == 128
            and hidden.shape[1] == CHUNKS * 8 * SUB_REQ * 4
            and hidden.shape[1] == 4 * cache.shape[0]
        )
        run = fast_shards if fits else plain_shards
        return run(hidden, w_qkv, cache, cache_len, receive)

    return jax.shard_map(
        shards,
        mesh=mesh,
        in_specs=(
            P("group", "seq", "mp"),
            P("mp", None, None),
            P("seq", None, "mp", None),
            P("seq"),
            P("seq"),
        ),
        out_specs=P("group", "seq", "mp"),
        check_vma=False,
    )
```

profile of v0, /device:TPU:5, one launch (start us, length us, event | category | flops | bytes accessed | tf_op | source)
XLA Modules:
  0.0 224.1 jit_solution(17999717949827500219)
XLA Ops:
  0.0 3.3 %slice_bitcast_fusion = (bf16[256,2048]{1,0:T(8,128)(2,1)}, bf16[256,2048]{1,0:T(8,128)(2,1)}) fusion(bf16[1,512,2048]{2,1,0:T(8,128)(2,1)} %param.5), kind=kLoop, calls=%fused_computation.1 | loop fusion | bytes 4194304 | tf_op jit(solution)/shard_map/slice | solution.py:584
  3.3 1.2 collective-permute-start.1
  5.5 23.0 %copy.13 = bf16[128,128,4,256]{3,1,0,2:T(8,128)(2,1)} copy(bf16[128,128,4,256]{3,2,1,0:T(4,128)(2,1)} %param.7) | data formatting | bytes 67108864 | tf_op args[2]
  30.1 1.2 collective-permute-start.3
  32.6 1.0 copy-done.8
  33.6 13.7 %project.2 = (bf16[2,4,1024,128]{3,2,1,0:T(8,128)(2,1)}, bf16[2,256,768]{2,1,0:T(8,128)(2,1)}, bf16[2,256,256]{2,1,0:T(8,128)(2,1)}, f32[2,8,128]{2,1,0:T(8,128)...) custom-call(s32[4]{0:T(128)} %pad_add_fusion.ids, bf16[512,2048]{1,0:T(8,128)(2,1)} %bitcast.18, ...), custom_call_target="tpu_custom_call" | custom-call | flops 1000 | bytes 1000 | tf_op jit(solution)/shard_map/project/pallas_call | solution.py:55
  47.3 7.9 %collective-permute-done.3.refs_0_ = bf16[256,2048]{1,0:T(8,128)(2,1)} collective-permute-done((bf16[256,2048]{1,0:T(8,128)(2,1)}, bf16[256,2048]{1,0:T(8,128)(2,1)}, u32[]{:S(2)}, u32[]{:S(2)}) %collective-permute-start.3) | collective-permute-done | bytes 1048608 | tf_op jit(solution)/shard_map/ppermute | solution.py:584
  55.9 1.3 collective-permute-start.5
  57.2 1.2 collective-permute-done.4.oth_s
  59.4 13.9 %project.3 = (bf16[2,4,1024,128]{3,2,1,0:T(8,128)(2,1)}, bf16[2,256,768]{2,1,0:T(8,128)(2,1)}, bf16[2,256,256]{2,1,0:T(8,128)(2,1)}, f32[2,8,128]{2,1,0:T(8,128)...) custom-call(s32[4]{0:T(128)} %pad_add_fusion.ids, ...), custom_call_target="tpu_custom_call", output_to_operand_aliasing={{0}: (6, {})} | custom-call | flops 199999995904 | bytes 1000 | tf_op jit(solution)/shard_map/project/pallas_call | solution.py:55
  73.4 1.3 collective-permute-start.13
  75.1 1.7 broadcast_select_fusion.1.refs_7_
  76.8 1.4 collective-permute-start.6
  79.0 4.3 %collective-permute-done.13 = bf16[528,256]{1,0:T(8,128)(2,1)S(1)} collective-permute-done((bf16[528,256]{1,0:T(8,128)(2,1)}, bf16[528,256]{1,0:T(8,128)(2,1)S(1)}, u32[]{:S(2)}, u32[]{:S(2)}) %collective-permute-start.13) | collective-permute-done | bytes 270368 | tf_op jit(solution)/shard_map/ppermute | solution.py:602
  84.2 8.1 %cache_attention.4.refs_1_.refs_23_ = f32[2,256,640]{2,1,0:T(8,128)S(1)} custom-call(s32[4]{0:T(128)S(1)} %copy-done, s32[128]{0:T(128)S(1)} %copy-done.2, s32[128]{0:T(128)S(1)} %copy-done.3, bf16[4,128,128,256]{3,2,1,0:T(8,128)(2,1)} %bitcast.14, bf16[2,4,1024,128]{3,2,1,0:T(8,128)(2,1)} %get-tuple-element.23.refs_0_.refs_2_, ...), custom_call_target="tpu_custom_call" | custom-call | flops 199999995904 | bytes 1000 | tf_op jit(solution)/shard_map/cache_attention/pallas_call | solution.py:55
  92.3 1.0 copy-done.5
  93.4 1.2 collective-permute-start.18
  94.8 1.2 collective-permute-start.11
  96.3 8.7 %cache_attention.5.refs_1_ = f32[2,256,640]{2,1,0:T(8,128)} custom-call(s32[4]{0:T(128)S(1)} %copy-done, s32[128]{0:T(128)S(1)} %copy-done.2, s32[128]{0:T(128)S(1)} %copy-done.3, bf16[4,128,128,256]{3,2,1,0:T(8,128)(2,1)} %bitcast.15, bf16[2,256,768]{2,1,0:T(8,128)(2,1)} %collective-permute-done.21.refs_0_, f32[2,256,640]{2,1,0:T(8,128)} %copy-done.5), custom_call_target="tpu_custom_call" | custom-call | flops 199999995904 | bytes 1000 | tf_op jit(solution)/shard_map/cache_attention/pallas_call | solution.py:55
  105.0 3.4 %collective-permute-start.22 = (f32[2,256,640]{2,1,0:T(8,128)}, f32[2,256,640]{2,1,0:T(8,128)}, u32[]{:S(2)}, u32[]{:S(2)}) collective-permute-start(f32[2,256,640]{2,1,0:T(8,128)} %cache_attention.5.refs_1_), channel_id=1, source_target_pairs={{0,2},{2,0},{4,6},{6,4},{8,10},{10,8},{12,14},{14,12},{1,3},{3,1},... | collective-permute-start | bytes 3932168 | tf_op jit(solution)/shard_map/ppermute | solution.py:572
  108.5 1.1 collective-permute-start.19
  109.9 1.1 collective-permute-start.12
  111.4 8.7 %cache_attention.6.refs_2_ = f32[2,256,640]{2,1,0:T(8,128)} custom-call(s32[4]{0:T(128)S(1)} %copy-done, s32[128]{0:T(128)S(1)} %copy-done.2, s32[128]{0:T(128)S(1)} %copy-done.3, bf16[4,128,128,256]{3,2,1,0:T(8,128)(2,1)} %bitcast.16, bf16[2,256,768]{2,1,0:T(8,128)(2,1)} %collective-permute-done.23.refs_0_, f32[2,256,640]{2,1,0:T(8,128)} %cache_attention.5.refs_1_), custom_call_target="tpu_custom_call" | custom-call | flops 199999995904 | bytes 1000 | tf_op jit(solution)/shard_map/cache_attention/pallas_call | solution.py:55
  120.1 1.4 collective-permute-start.24
  121.5 1.1 collective-permute-start.20
  123.6 8.1 %cache_attention.7.refs_25_ = f32[2,256,640]{2,1,0:T(8,128)S(1)} custom-call(s32[4]{0:T(128)S(1)} %copy-done, s32[128]{0:T(128)S(1)} %copy-done.2, s32[128]{0:T(128)S(1)} %copy-done.3, bf16[4,128,128,256]{3,2,1,0:T(8,128)(2,1)} %bitcast.17, bf16[2,4,1024,128]{3,2,1,0:T(8,128)(2,1)} %get-tuple-element.23.refs_0_.refs_2_, ...), custom_call_target="tpu_custom_call" | custom-call | flops 199999995904 | bytes 1000 | tf_op jit(solution)/shard_map/cache_attention/pallas_call | solution.py:55
  131.7 1.1 copy-done.4
  132.8 3.2 %collective-permute-done.17.refs_19_ = bf16[528,256]{1,0:T(8,128)(2,1)} collective-permute-done((bf16[528,256]{1,0:T(8,128)(2,1)}, bf16[528,256]{1,0:T(8,128)(2,1)}, u32[]{:S(2)}, u32[]{:S(2)}) %collective-permute-start.17) | collective-permute-done | bytes 270368 | tf_op jit(solution)/shard_map/ppermute | solution.py:577
  135.9 80.3 %prompt_attention.1 = (bf16[512,2048]{1,0:T(8,128)(2,1)}, bf16[512,1024]{1,0:T(8,128)(2,1)}) custom-call(s32[4]{0:T(128)} %pad_add_fusion.ids, f32[2,8,128]{2,1,0:T(8,128)} %get-tuple-element.19.refs_0_, f32[2,8,128]{2,1,0:T(8,128)} %get-tuple-element.22.refs_1_, bf16[2,4,1024,128]{3,2,1,0:T(8,128)(2,1)} %get-tuple-element.23.refs_0_.refs_2_, ...), custom_call_target="tpu_custom_call" | custom-call | flops 199999995904 | bytes 1000 | tf_op jit(solution)/shard_map/prompt_attention/pallas_call | solution.py:55
  216.2 1.8 collective-permute-start.25
  218.0 2.5 %collective-permute-done.25.back = bf16[512,1024]{1,0:T(8,128)(2,1)S(1)} collective-permute-done((bf16[512,1024]{1,0:T(8,128)(2,1)}, bf16[512,1024]{1,0:T(8,128)(2,1)S(1)}, u32[]{:S(2)}, u32[]{:S(2)}) %collective-permute-start.25) | collective-permute-done | bytes 1048608 | tf_op jit(solution)/shard_map/ppermute | solution.py:572
  221.5 2.6 %fill_other_half.1 = bf16[512,2048]{1,0:T(8,128)(2,1)} custom-call(s32[4]{0:T(128)S(1)} %copy-done.1, bf16[512,2048]{1,0:T(8,128)(2,1)} %get-tuple-element.31.out_before, bf16[512,1024]{1,0:T(8,128)(2,1)} %copy-done.9), custom_call_target="tpu_custom_call", output_to_operand_aliasing={{}: (1, {})} | custom-call | flops 1000 | bytes 1000 | tf_op jit(solution)/shard_map/fill_other_half/pallas_call | solution.py:55
  (60 shorter events, 10.8 us)
Async XLA Ops:
  0.0 4.5 %copy-start.6 = (bf16[1,512,2048]{2,1,0:T(8,128)(2,1)S(1)}, bf16[1,512,2048]{2,1,0:T(8,128)(2,1)}, u32[]{:S(2)}) copy-start(bf16[1,512,2048]{2,1,0:T(8,128)(2,1)} %param.5) | copy-start | bytes 6291460
  3.3 25.2 %collective-permute-start.1 = (bf16[256,2048]{1,0:T(8,128)(2,1)}, bf16[256,2048]{1,0:T(8,128)(2,1)S(1)}, u32[]{:S(2)}, u32[]{:S(2)}) collective-permute-start(bf16[256,2048]{1,0:T(8,128)(2,1)} %get-tuple-element.34), channel_id=1, source_target_pairs={{0,1},{1,0},{2,3},{3,2},{4,5},{5,4},{6,7},{7,6},{8,9},{9,8},{10,11... | collective-permute-start | bytes 3145736 | tf_op jit(solution)/shard_map/ppermute | solution.py:584
  4.5 28.1 %collective-permute-start = (bf16[512,2048]{1,0:T(8,128)(2,1)S(1)}, bf16[512,2048]{1,0:T(8,128)(2,1)}, u32[]{:S(2)}, u32[]{:S(2)}) collective-permute-start(bf16[512,2048]{1,0:T(8,128)(2,1)S(1)} %bitcast.20), channel_id=1, source_target_pairs={{0,2},{2,0},{4,6},{6,4},{8,10},{10,8},{12,14},{14,12},{1,3},{3,1},... | collective-permute-start | bytes 6291464 | tf_op jit(solution)/shard_map/ppermute | solution.py:572
  29.5 3.1 %collective-permute-start.2 = (bf16[256,2048]{1,0:T(8,128)(2,1)}, bf16[256,2048]{1,0:T(8,128)(2,1)S(1)}, u32[]{:S(2)}, u32[]{:S(2)}) collective-permute-start(bf16[256,2048]{1,0:T(8,128)(2,1)} %after_all.3.oth), channel_id=1, source_target_pairs={{0,2},{2,0},{4,6},{6,4},{8,10},{10,8},{12,14},{14,12},{1,3},{3,1},... | collective-permute-start | bytes 3145736 | tf_op jit(solution)/shard_map/ppermute | solution.py:572
  30.1 25.1 %collective-permute-start.3 = (bf16[256,2048]{1,0:T(8,128)(2,1)}, bf16[256,2048]{1,0:T(8,128)(2,1)}, u32[]{:S(2)}, u32[]{:S(2)}) collective-permute-start(bf16[256,2048]{1,0:T(8,128)(2,1)} %get-tuple-element.33), channel_id=1, source_target_pairs={{0,1},{1,0},{2,3},{3,2},{4,5},{5,4},{6,7},{7,6},{8,9},{9,8},{10,11... | collective-permute-start | bytes 3145736 | tf_op jit(solution)/shard_map/ppermute | solution.py:584
  55.2 3.3 %collective-permute-start.4 = (bf16[256,2048]{1,0:T(8,128)(2,1)}, bf16[256,2048]{1,0:T(8,128)(2,1)S(1)}, u32[]{:S(2)}, u32[]{:S(2)}) collective-permute-start(bf16[256,2048]{1,0:T(8,128)(2,1)} %after_all.4.oth), channel_id=1, source_target_pairs={{0,2},{2,0},{4,6},{6,4},{8,10},{10,8},{12,14},{14,12},{1,3},{3,1},... | collective-permute-start | bytes 3145736 | tf_op jit(solution)/shard_map/ppermute | solution.py:572
  55.9 19.1 %collective-permute-start.5 = (bf16[528,256]{1,0:T(8,128)(2,1)}, bf16[528,256]{1,0:T(8,128)(2,1)}, u32[]{:S(2)}, u32[]{:S(2)}) collective-permute-start(bf16[528,256]{1,0:T(8,128)(2,1)} %get-tuple-element.25.refs_4_), channel_id=1, source_target_pairs={{0,16},{1,17},{2,18},{3,19},{4,20},{5,21},{6,22},{7,23},{8,24},{9,... | collective-permute-start | bytes 811016 | tf_op jit(solution)/shard_map/ppermute | solution.py:597
  59.4 15.7 %copy-start.10 = (bf16[528,256]{1,0:T(8,128)(2,1)S(1)}, bf16[528,256]{1,0:T(8,128)(2,1)}, u32[]{:S(2)}) copy-start(bf16[528,256]{1,0:T(8,128)(2,1)} %get-tuple-element.24.refs_3_) | copy-start | bytes 811012
  73.3 10.9 %copy-start = (s32[4]{0:T(128)S(1)}, s32[4]{0:T(128)}, u32[]{:S(2)}) copy-start(s32[4]{0:T(128)} %pad_add_fusion.ids) | copy-start | bytes 52
  73.3 10.9 %copy-start.2 = (s32[128]{0:T(128)S(1)}, s32[128]{0:T(128)}, u32[]{:S(2)}) copy-start(s32[128]{0:T(128)} %lens.7) | copy-start | bytes 1540
  73.3 10.9 %copy-start.3 = (s32[128]{0:T(128)S(1)}, s32[128]{0:T(128)}, u32[]{:S(2)}) copy-start(s32[128]{0:T(128)} %receive.7) | copy-start | bytes 1540
  73.4 9.9 %collective-permute-start.13 = (bf16[528,256]{1,0:T(8,128)(2,1)}, bf16[528,256]{1,0:T(8,128)(2,1)S(1)}, u32[]{:S(2)}, u32[]{:S(2)}) collective-permute-start(bf16[528,256]{1,0:T(8,128)(2,1)} %get-tuple-element.27.refs_6_), channel_id=1, source_target_pairs={{0,16},{1,17},{2,18},{3,19},{4,20},{5,21},{6,22},{7,23},{8,24},{9,... | collective-permute-start | bytes 811016 | tf_op jit(solution)/shard_map/ppermute | solution.py:602
  74.7 18.7 %collective-permute-start.21 = (bf16[2,256,768]{2,1,0:T(8,128)(2,1)}, bf16[2,256,768]{2,1,0:T(8,128)(2,1)}, u32[]{:S(2)}, u32[]{:S(2)}) collective-permute-start(bf16[2,256,768]{2,1,0:T(8,128)(2,1)} %get-tuple-element.29), channel_id=1, source_target_pairs={{0,2},{2,0},{4,6},{6,4},{8,10},{10,8},{12,14},{14,12},{1,3},{3,1},... | collective-permute-start | bytes 2359304 | tf_op jit(solution)/shard_map/ppermute | solution.py:572
  76.8 17.8 %collective-permute-start.6 = (bf16[528,256]{1,0:T(8,128)(2,1)}, bf16[528,256]{1,0:T(8,128)(2,1)}, u32[]{:S(2)}, u32[]{:S(2)}) collective-permute-start(bf16[528,256]{1,0:T(8,128)(2,1)} %broadcast_select_fusion.1.refs_7_), channel_id=1, source_target_pairs={{0,4},{2,6},{4,8},{6,10},{8,12},{10,14},{12,28},{14,30},{28,24},{3... | collective-permute-start | bytes 811016 | tf_op jit(solution)/shard_map/ppermute | solution.py:577
  78.2 16.6 %collective-permute-start.10 = (bf16[528,256]{1,0:T(8,128)(2,1)}, bf16[528,256]{1,0:T(8,128)(2,1)}, u32[]{:S(2)}, u32[]{:S(2)}) collective-permute-start(bf16[528,256]{1,0:T(8,128)(2,1)} %broadcast_select_fusion.1.refs_7_), channel_id=1, source_target_pairs={{0,16},{2,18},{4,0},{6,2},{8,4},{10,6},{12,8},{14,10},{28,12},{30,... | collective-permute-start | bytes 811016 | tf_op jit(solution)/shard_map/ppermute | solution.py:579
  78.3 31.6 %collective-permute-start.23 = (bf16[2,256,768]{2,1,0:T(8,128)(2,1)}, bf16[2,256,768]{2,1,0:T(8,128)(2,1)}, u32[]{:S(2)}, u32[]{:S(2)}) collective-permute-start(bf16[2,256,768]{2,1,0:T(8,128)(2,1)} %get-tuple-element.30), channel_id=1, source_target_pairs={{0,2},{2,0},{4,6},{6,4},{8,10},{10,8},{12,14},{14,12},{1,3},{3,1},... | collective-permute-start | bytes 2359304 | tf_op jit(solution)/shard_map/ppermute | solution.py:572
  84.0 12.1 %collective-permute-start.14 = (bf16[528,256]{1,0:T(8,128)(2,1)}, bf16[528,256]{1,0:T(8,128)(2,1)}, u32[]{:S(2)}, u32[]{:S(2)}) collective-permute-start(bf16[528,256]{1,0:T(8,128)(2,1)} %broadcast_select_fusion.refs_15_), channel_id=1, source_target_pairs={{0,4},{2,6},{4,8},{6,10},{8,12},{10,14},{12,28},{14,30},{28,24},{3... | collective-permute-start | bytes 811016 | tf_op jit(solution)/shard_map/ppermute | solution.py:577
  93.4 11.7 %collective-permute-start.18 = (bf16[528,256]{1,0:T(8,128)(2,1)}, bf16[528,256]{1,0:T(8,128)(2,1)}, u32[]{:S(2)}, u32[]{:S(2)}) collective-permute-start(bf16[528,256]{1,0:T(8,128)(2,1)} %broadcast_select_fusion.refs_15_), channel_id=1, source_target_pairs={{0,16},{2,18},{4,0},{6,2},{8,4},{10,6},{12,8},{14,10},{28,12},{30,... | collective-permute-start | bytes 811016 | tf_op jit(solution)/shard_map/ppermute | solution.py:579
  94.6 13.8 %collective-permute-start.7 = (bf16[528,256]{1,0:T(8,128)(2,1)}, bf16[528,256]{1,0:T(8,128)(2,1)}, u32[]{:S(2)}, u32[]{:S(2)}) collective-permute-start(bf16[528,256]{1,0:T(8,128)(2,1)} %collective-permute-done.6.refs_8_), channel_id=1, source_target_pairs={{0,4},{2,6},{4,8},{6,10},{8,12},{10,14},{12,28},{14,30},{28,24},{3... | collective-permute-start | bytes 811016 | tf_op jit(solution)/shard_map/ppermute | solution.py:577
  94.8 14.8 %collective-permute-start.11 = (bf16[528,256]{1,0:T(8,128)(2,1)}, bf16[528,256]{1,0:T(8,128)(2,1)}, u32[]{:S(2)}, u32[]{:S(2)}) collective-permute-start(bf16[528,256]{1,0:T(8,128)(2,1)} %collective-permute-done.10.refs_14_), channel_id=1, source_target_pairs={{0,16},{2,18},{4,0},{6,2},{8,4},{10,6},{12,8},{14,10},{28,12},{30,... | collective-permute-start | bytes 811016 | tf_op jit(solution)/shard_map/ppermute | solution.py:579
  96.1 15.0 %collective-permute-start.15 = (bf16[528,256]{1,0:T(8,128)(2,1)}, bf16[528,256]{1,0:T(8,128)(2,1)}, u32[]{:S(2)}, u32[]{:S(2)}) collective-permute-start(bf16[528,256]{1,0:T(8,128)(2,1)} %collective-permute-done.14.refs_16_), channel_id=1, source_target_pairs={{0,4},{2,6},{4,8},{6,10},{8,12},{10,14},{12,28},{14,30},{28,24},{3... | collective-permute-start | bytes 811016 | tf_op jit(solution)/shard_map/ppermute | solution.py:577
  105.0 27.7 %collective-permute-start.22 = (f32[2,256,640]{2,1,0:T(8,128)}, f32[2,256,640]{2,1,0:T(8,128)}, u32[]{:S(2)}, u32[]{:S(2)}) collective-permute-start(f32[2,256,640]{2,1,0:T(8,128)} %cache_attention.5.refs_1_), channel_id=1, source_target_pairs={{0,2},{2,0},{4,6},{6,4},{8,10},{10,8},{12,14},{14,12},{1,3},{3,1},... | collective-permute-start | bytes 3932168 | tf_op jit(solution)/shard_map/ppermute | solution.py:572
  108.5 11.7 %collective-permute-start.19 = (bf16[528,256]{1,0:T(8,128)(2,1)}, bf16[528,256]{1,0:T(8,128)(2,1)}, u32[]{:S(2)}, u32[]{:S(2)}) collective-permute-start(bf16[528,256]{1,0:T(8,128)(2,1)} %collective-permute-done.18.refs_22_), channel_id=1, source_target_pairs={{0,16},{2,18},{4,0},{6,2},{8,4},{10,6},{12,8},{14,10},{28,12},{30,... | collective-permute-start | bytes 811016 | tf_op jit(solution)/shard_map/ppermute | solution.py:579
  109.6 11.9 %collective-permute-start.8 = (bf16[528,256]{1,0:T(8,128)(2,1)}, bf16[528,256]{1,0:T(8,128)(2,1)}, u32[]{:S(2)}, u32[]{:S(2)}) collective-permute-start(bf16[528,256]{1,0:T(8,128)(2,1)} %collective-permute-done.7.refs_9_), channel_id=1, source_target_pairs={{0,4},{2,6},{4,8},{6,10},{8,12},{10,14},{12,28},{14,30},{28,24},{3... | collective-permute-start | bytes 811016 | tf_op jit(solution)/shard_map/ppermute | solution.py:577
  109.9 12.7 %collective-permute-start.12 = (bf16[528,256]{1,0:T(8,128)(2,1)}, bf16[528,256]{1,0:T(8,128)(2,1)}, u32[]{:S(2)}, u32[]{:S(2)}) collective-permute-start(bf16[528,256]{1,0:T(8,128)(2,1)} %collective-permute-done.11.refs_13_), channel_id=1, source_target_pairs={{0,16},{2,18},{4,0},{6,2},{8,4},{10,6},{12,8},{14,10},{28,12},{30,... | collective-permute-start | bytes 811016 | tf_op jit(solution)/shard_map/ppermute | solution.py:579
  111.1 12.2 %collective-permute-start.16 = (bf16[528,256]{1,0:T(8,128)(2,1)}, bf16[528,256]{1,0:T(8,128)(2,1)}, u32[]{:S(2)}, u32[]{:S(2)}) collective-permute-start(bf16[528,256]{1,0:T(8,128)(2,1)} %collective-permute-done.15.refs_17_), channel_id=1, source_target_pairs={{0,4},{2,6},{4,8},{6,10},{8,12},{10,14},{12,28},{14,30},{28,24},{3... | collective-permute-start | bytes 811016 | tf_op jit(solution)/shard_map/ppermute | solution.py:577
  120.1 15.8 %collective-permute-start.24 = (f32[2,256,640]{2,1,0:T(8,128)}, f32[2,256,640]{2,1,0:T(8,128)}, u32[]{:S(2)}, u32[]{:S(2)}) collective-permute-start(f32[2,256,640]{2,1,0:T(8,128)} %cache_attention.6.refs_2_), channel_id=1, source_target_pairs={{0,2},{2,0},{4,6},{6,4},{8,10},{10,8},{12,14},{14,12},{1,3},{3,1},... | collective-permute-start | bytes 3932168 | tf_op jit(solution)/shard_map/ppermute | solution.py:572
  121.5 11.3 %collective-permute-start.20 = (bf16[528,256]{1,0:T(8,128)(2,1)}, bf16[528,256]{1,0:T(8,128)(2,1)}, u32[]{:S(2)}, u32[]{:S(2)}) collective-permute-start(bf16[528,256]{1,0:T(8,128)(2,1)} %collective-permute-done.19.refs_21_), channel_id=1, source_target_pairs={{0,16},{2,18},{4,0},{6,2},{8,4},{10,6},{12,8},{14,10},{28,12},{30,... | collective-permute-start | bytes 811016 | tf_op jit(solution)/shard_map/ppermute | solution.py:579
  122.6 10.1 %collective-permute-start.9 = (bf16[528,256]{1,0:T(8,128)(2,1)}, bf16[528,256]{1,0:T(8,128)(2,1)}, u32[]{:S(2)}, u32[]{:S(2)}) collective-permute-start(bf16[528,256]{1,0:T(8,128)(2,1)} %collective-permute-done.8.refs_10_), channel_id=1, source_target_pairs={{0,4},{2,6},{4,8},{6,10},{8,12},{10,14},{12,28},{14,30},{28,24},{3... | collective-permute-start | bytes 811016 | tf_op jit(solution)/shard_map/ppermute | solution.py:577
  123.2 12.7 %collective-permute-start.17 = (bf16[528,256]{1,0:T(8,128)(2,1)}, bf16[528,256]{1,0:T(8,128)(2,1)}, u32[]{:S(2)}, u32[]{:S(2)}) collective-permute-start(bf16[528,256]{1,0:T(8,128)(2,1)} %collective-permute-done.16.refs_18_), channel_id=1, source_target_pairs={{0,4},{2,6},{4,8},{6,10},{8,12},{10,14},{12,28},{14,30},{28,24},{3... | collective-permute-start | bytes 811016 | tf_op jit(solution)/shard_map/ppermute | solution.py:577
  135.9 85.5 %copy-start.1 = (s32[4]{0:T(128)S(1)}, s32[4]{0:T(128)}, u32[]{:S(2)}) copy-start(s32[4]{0:T(128)} %pad_add_fusion.ids) | copy-start | bytes 52
  216.2 4.3 %collective-permute-start.25 = (bf16[512,1024]{1,0:T(8,128)(2,1)}, bf16[512,1024]{1,0:T(8,128)(2,1)S(1)}, u32[]{:S(2)}, u32[]{:S(2)}) collective-permute-start(bf16[512,1024]{1,0:T(8,128)(2,1)} %get-tuple-element.32), channel_id=1, source_target_pairs={{0,2},{2,0},{4,6},{6,4},{8,10},{10,8},{12,14},{14,12},{1,3},{3,1},... | collective-permute-start | bytes 3145736 | tf_op jit(solution)/shard_map/ppermute | solution.py:572
  (6 other events, 6.1 us)
where the time goes:
time: 225 us; the launch traced here: 224 us
  Pallas kernels  144 us (64%)
  local copies, waits for them, and re-layouts  32.4 us (14%)
  starting transfers between devices  24.3 us (11%)
  waiting for transfers between devices  20 us (9%)
  other arithmetic  3.09 us (1%)
    pallas_call x8, Pallas kernels, on(): return made(*args[:prefetch], *kept)  144 us
    unnamed x25, local copies, waits for them, and re-layouts  29.2 us
    ppermute x8, starting transfers between devices, swap_cores(): return lax.ppermute(x, 'seq', core_swap)  10 us
    ppermute x2, waiting for transfers between devices, fast_shards(): lax.ppermute(own[c * rows:(c + 1) * rows], 'mp', mp_swap)  7.88 us
    ppermute x6, starting transfers between devices, round_the_ring(): downs.append(lax.ppermute(downs[-1], ('group', 'seq'), down))  5.98 us
  transfers between devices with their start and end apart: 26, of which 7 were waited for; matrix products, arithmetic and copies ran while one was open for 12% of the time, Pallas kernels for 27%

commit v1 on v0

--- a/solution.py
+++ b/solution.py
@@ -31,7 +31,7 @@
     return lax.dot_general(a, b, dims, preferred_element_type=jnp.float32)
 
 
-def call(kernel, name, grid, prefetch, in_specs, out_specs, out_shape, scratch=(), cost=SMALL, mib=48, aliases=None):
+def call(kernel, name, grid, prefetch, in_specs, out_specs, out_shape, scratch=(), cost=SMALL, mib=48, aliases=None, free=()):
     made = pl.pallas_call(
         kernel,
         grid_spec=pltpu.PrefetchScalarGridSpec(
@@ -51,8 +51,11 @@
     )
 
     def on(*args):
-        kept = [pltpu.with_memory_space_constraint(x, pltpu.HBM) for x in args[prefetch:]]
-        return made(*args[:prefetch], *kept)
+        kept = [
+            x if i < prefetch or i in free else pltpu.with_memory_space_constraint(x, pltpu.HBM)
+            for i, x in enumerate(args)
+        ]
+        return made(*kept)
 
     return on
 
@@ -60,12 +63,29 @@
 def after_all(block, *before):
     return pl.pallas_call(
         lambda *refs: None,
-        in_specs=[ANY] * (1 + len(before)),
-        out_specs=ANY,
+        in_specs=[pl.BlockSpec(memory_space=pl.ANY)] * (1 + len(before)),
+        out_specs=pl.BlockSpec(memory_space=pl.ANY),
         out_shape=jax.ShapeDtypeStruct(block.shape, block.dtype),
         input_output_aliases={0: 0},
         name="after_all",
     )(block, *before)
+
+
+def take_kernel(ids, x, *refs):
+    refs[-1][...] = x[...]
+
+
+def take_rows(x, chunk, rows, after):
+    block = (rows // 2, x.shape[1])
+    return call(
+        take_kernel,
+        "take_rows",
+        (2,),
+        1,
+        [pl.BlockSpec(block, lambda i, ids: (2 * chunk + i, 0))] + [ANY] * len(after),
+        pl.BlockSpec(block, lambda i, ids: (i, 0)),
+        jax.ShapeDtypeStruct((rows, x.shape[1]), x.dtype),
+    )(jnp.zeros((1,), jnp.int32), x, *after)
 
 
 def longest_row(x):
@@ -183,6 +203,7 @@
         cost=cost,
         mib=56,
         aliases=aliases,
+        free=(2, 3, 4),
     )(*args, *after)
 
 
@@ -524,6 +545,7 @@
         ],
         cost=LARGE,
         mib=58,
+        free=range(2 + 3 * CHUNKS + slots_n * CHUNKS, 2 + 3 * CHUNKS + slots_n * CHUNKS + len(parts)),
     )(ids, *norms, q, *own[0], *own[1], *arrived[0], *arrived[1], *parts, *after)
 
 
@@ -543,6 +565,7 @@
         pl.BlockSpec(block, lambda i, ids: (i, 1 - ids[0])),
         jax.ShapeDtypeStruct(out.shape, out.dtype),
         aliases={1: 0},
+        free=(2,),
     )(ids, out, back)
 
 
@@ -581,7 +604,10 @@
 
     prefill = group_i == 0
     own = hidden[0]
-    oth = [lax.ppermute(own[c * rows : (c + 1) * rows], "mp", mp_swap) for c in range(CHUNKS)]
+    pieces = []
+    for c in range(CHUNKS):
+        pieces.append(take_rows(own, c, rows, pieces[-1:]))
+    oth = [lax.ppermute(piece, "mp", mp_swap) for piece in pieces]
     own_s = swap_cores(own)
     cache_t = jnp.transpose(cache, (2, 0, 1, 3))
 
@@ -596,13 +622,13 @@
     q, theirs_0, kv_0, norms_0, kv0_0, kv1_0 = projected(0, None, SMALL)
     crossed_0 = lax.ppermute(kv1_0, "group", [(0, 1)])
     swapped_0 = swap_cores(theirs_0)
-    oth[1] = after_all(oth[1], kv_0)
+    near_0 = cached(0, 0, (q, kv_0), [])
+    oth[1] = after_all(oth[1], near_0)
 
     q, theirs_1, kv_1, norms_1, kv0_1, kv1_1 = projected(1, q, LARGE)
     crossed_1 = lax.ppermute(kv1_1, "group", [(0, 1)])
     swapped_1 = swap_cores(theirs_1)
     ring_0 = round_the_ring(jnp.where(prefill, kv0_0, after_all(crossed_0, kv_1)))
-    near_0 = cached(0, 0, (q, kv_0), [])
     ring_1 = round_the_ring(jnp.where(prefill, kv0_1, crossed_1))
     far_0 = cached(1, 0, (swapped_0,), [near_0])
     away_0 = swap_cores(far_0)

time: 225 us -> 220 us (0.978)
  local copies, waits for them, and re-layouts: 32.4 us -> 27.3 us
  waiting for transfers between devices: 20 us -> 16.3 us
  Pallas kernels: 144 us -> 147 us
    ppermute x2, waiting for transfers between devices: 7.88 us -> 0.01 us  [fast_shards(): oth = [lax.ppermute(piece, 'mp', mp_swap) for piece in pieces]]
    slice x1 -> x0, local copies, waits for them, and re-layouts: 3.28 us -> none  [fast_shards(): own[c * rows:(c + 1) * rows]]
    pallas_call x11 -> x13, Pallas kernels: 144 us -> 147 us  [the longest x10 147 us: on(): return made(*kept)]
    ppermute x8, waiting for transfers between devices: 3.45 us -> 5.78 us  [round_the_ring(): ups.append(lax.ppermute(ups[-1], ('group', 'seq'), up))]
    unnamed x25 -> x31, local copies, waits for them, and re-layouts: 29.2 us -> 27.3 us
  transfers between devices with their start and end apart: 26 -> 26, of which waited for: 7 -> 7; matrix products, arithmetic and copies ran while one was open for 12% -> 12% of each run, Pallas kernels for 27% -> 29%
where the time goes in v1:
time: 220 us; the launch traced here: 218 us
  Pallas kernels  147 us (67%)
  local copies, waits for them, and re-layouts  27.3 us (12%)
  starting transfers between devices  25.3 us (12%)
  waiting for transfers between devices  16.3 us (7%)
  other arithmetic  2.37 us (1%)
    pallas_call x10, Pallas kernels, on(): return made(*kept)  147 us
    unnamed x31, local copies, waits for them, and re-layouts  27.3 us
    ppermute x8, starting transfers between devices, swap_cores(): return lax.ppermute(x, 'seq', core_swap)  11.9 us
    ppermute x6, starting transfers between devices, round_the_ring(): downs.append(lax.ppermute(downs[-1], ('group', 'seq'), down))  5.84 us
    ppermute x8, waiting for transfers between devices, round_the_ring(): ups.append(lax.ppermute(ups[-1], ('group', 'seq'), up))  5.78 us
    ppermute x1, waiting for transfers between devices, fast_shards(): crossed_1 = lax.ppermute(kv1_1, 'group', [(0, 1)])  5.65 us
  transfers between devices with their start and end apart: 26, of which 7 were waited for; matrix products, arithmetic and copies ran while one was open for 12% of the time, Pallas kernels for 29%

profile of v1, /device:TPU:5, one launch (start us, length us, event | category | flops | bytes accessed | tf_op | source)
XLA Modules:
  0.0 218.1 jit_solution(3620511479813265551)
XLA Ops:
  0.0 1.4 take_rows.2.refs_0_
  1.4 1.3 collective-permute-start.1
  3.7 23.1 %copy.13 = bf16[128,128,4,256]{3,1,0,2:T(8,128)(2,1)} copy(bf16[128,128,4,256]{3,2,1,0:T(4,128)(2,1)} %param.7) | data formatting | bytes 67108864 | tf_op args[2]
  27.2 2.1 take_rows.3
  29.3 1.2 collective-permute-start.3
  32.1 13.7 %project.2 = (bf16[2,4,1024,128]{3,2,1,0:T(8,128)(2,1)}, bf16[2,256,768]{2,1,0:T(8,128)(2,1)}, bf16[2,256,256]{2,1,0:T(8,128)(2,1)}, f32[2,8,128]{2,1,0:T(8,128)...) custom-call(s32[4]{0:T(128)} %pad_add_fusion.ids, bf16[512,2048]{1,0:T(8,128)(2,1)} %bitcast.16, ...), custom_call_target="tpu_custom_call" | custom-call | flops 1000 | bytes 1000 | tf_op jit(solution)/shard_map/project/pallas_call | solution.py:58
  45.8 8.1 %cache_attention.4.refs_1_.refs_23_ = f32[2,256,640]{2,1,0:T(8,128)S(1)} custom-call(s32[4]{0:T(128)S(1)} %copy-done.2, s32[128]{0:T(128)S(1)} %copy-done.5, s32[128]{0:T(128)S(1)} %copy-done.7, bf16[4,128,128,256]{3,2,1,0:T(8,128)(2,1)} %bitcast.10, bf16[2,4,1024,128]{3,2,1,0:T(8,128)(2,1)} %get-tuple-element.20.refs_0_, ...), custom_call_target="tpu_custom_call" | custom-call | flops 199999995904 | bytes 1000 | tf_op jit(solution)/shard_map/cache_attention/pallas_call | solution.py:58
  53.9 1.1 copy-done.1
  55.5 1.3 collective-permute-start.5
  56.8 1.1 collective-permute-done.4.oth_s
  58.9 13.9 %project.3 = (bf16[2,4,1024,128]{3,2,1,0:T(8,128)(2,1)}, bf16[2,256,768]{2,1,0:T(8,128)(2,1)}, bf16[2,256,256]{2,1,0:T(8,128)(2,1)}, f32[2,8,128]{2,1,0:T(8,128)...) custom-call(s32[4]{0:T(128)} %pad_add_fusion.ids, ...), custom_call_target="tpu_custom_call", output_to_operand_aliasing={{0}: (6, {})} | custom-call | flops 199999995904 | bytes 1000 | tf_op jit(solution)/shard_map/project/pallas_call | solution.py:58
  72.8 1.3 collective-permute-start.13
  75.2 1.2 collective-permute-start.6
  77.1 5.7 %collective-permute-done.13 = bf16[528,256]{1,0:T(8,128)(2,1)S(1)} collective-permute-done((bf16[528,256]{1,0:T(8,128)(2,1)}, bf16[528,256]{1,0:T(8,128)(2,1)S(1)}, u32[]{:S(2)}, u32[]{:S(2)}) %collective-permute-start.13) | collective-permute-done | bytes 270368 | tf_op jit(solution)/shard_map/ppermute | solution.py:629
  83.8 2.1 collective-permute-start.23
  85.9 1.1 collective-permute-start.18
  87.3 1.3 collective-permute-done.10.refs_14_
  88.6 1.5 collective-permute-done.14.refs_16_
  90.2 8.7 %cache_attention.5.refs_1_ = f32[2,256,640]{2,1,0:T(8,128)} custom-call(s32[4]{0:T(128)S(1)} %copy-done.3, s32[128]{0:T(128)S(1)} %copy-done.6, s32[128]{0:T(128)S(1)} %copy-done.8, bf16[4,128,128,256]{3,2,1,0:T(8,128)(2,1)} %bitcast.11, bf16[2,256,768]{2,1,0:T(8,128)(2,1)} %collective-permute-done.21.refs_0_, f32[2,256,640]{2,1,0:T(8,128)} %copy-done.1), custom_call_target="tpu_custom_call" | custom-call | flops 199999995904 | bytes 1000 | tf_op jit(solution)/shard_map/cache_attention/pallas_call | solution.py:58
  99.0 5.2 %collective-permute-start.22 = (f32[2,256,640]{2,1,0:T(8,128)}, f32[2,256,640]{2,1,0:T(8,128)}, u32[]{:S(2)}, u32[]{:S(2)}) collective-permute-start(f32[2,256,640]{2,1,0:T(8,128)} %cache_attention.5.refs_1_), channel_id=1, source_target_pairs={{0,2},{2,0},{4,6},{6,4},{8,10},{10,8},{12,14},{14,12},{1,3},{3,1},... | collective-permute-start | bytes 3932168 | tf_op jit(solution)/shard_map/ppermute | solution.py:595
  104.2 1.3 collective-permute-start.19
  105.7 1.3 collective-permute-start.12
  107.1 8.7 %cache_attention.6.refs_2_ = f32[2,256,640]{2,1,0:T(8,128)} custom-call(s32[4]{0:T(128)S(1)} %copy-done.3, s32[128]{0:T(128)S(1)} %copy-done.6, s32[128]{0:T(128)S(1)} %copy-done.8, bf16[4,128,128,256]{3,2,1,0:T(8,128)(2,1)} %bitcast.12, bf16[2,256,768]{2,1,0:T(8,128)(2,1)} %collective-permute-done.23.refs_0_, f32[2,256,640]{2,1,0:T(8,128)} %cache_attention.5.refs_1_), custom_call_target="tpu_custom_call" | custom-call | flops 199999995904 | bytes 1000 | tf_op jit(solution)/shard_map/cache_attention/pallas_call | solution.py:58
  115.9 1.2 collective-permute-start.24
  117.1 1.3 collective-permute-start.20
  119.5 8.1 %cache_attention.7.refs_25_ = f32[2,256,640]{2,1,0:T(8,128)S(1)} custom-call(s32[4]{0:T(128)S(1)} %copy-done.3, s32[128]{0:T(128)S(1)} %copy-done.6, s32[128]{0:T(128)S(1)} %copy-done.8, bf16[4,128,128,256]{3,2,1,0:T(8,128)(2,1)} %bitcast.13, bf16[2,4,1024,128]{3,2,1,0:T(8,128)(2,1)} %get-tuple-element.23.refs_0_.refs_2_, ...), custom_call_target="tpu_custom_call" | custom-call | flops 199999995904 | bytes 1000 | tf_op jit(solution)/shard_map/cache_attention/pallas_call | solution.py:58
  127.6 1.1 copy-done.9
  128.7 3.4 %collective-permute-done.17.refs_19_ = bf16[528,256]{1,0:T(8,128)(2,1)} collective-permute-done((bf16[528,256]{1,0:T(8,128)(2,1)}, bf16[528,256]{1,0:T(8,128)(2,1)}, u32[]{:S(2)}, u32[]{:S(2)}) %collective-permute-start.17) | collective-permute-done | bytes 270368 | tf_op jit(solution)/shard_map/ppermute | solution.py:600
  132.1 80.3 %prompt_attention.1 = (bf16[512,2048]{1,0:T(8,128)(2,1)}, bf16[512,1024]{1,0:T(8,128)(2,1)}) custom-call(s32[4]{0:T(128)} %pad_add_fusion.ids, f32[2,8,128]{2,1,0:T(8,128)} %get-tuple-element.19.refs_0_, f32[2,8,128]{2,1,0:T(8,128)} %get-tuple-element.22.refs_1_, bf16[2,4,1024,128]{3,2,1,0:T(8,128)(2,1)} %get-tuple-element.23.refs_0_.refs_2_, ...), custom_call_target="tpu_custom_call" | custom-call | flops 199999995904 | bytes 1000 | tf_op jit(solution)/shard_map/prompt_attention/pallas_call | solution.py:58
  212.4 1.6 collective-permute-start.25
  214.0 2.5 %collective-permute-done.25.back = bf16[512,1024]{1,0:T(8,128)(2,1)S(1)} collective-permute-done((bf16[512,1024]{1,0:T(8,128)(2,1)}, bf16[512,1024]{1,0:T(8,128)(2,1)S(1)}, u32[]{:S(2)}, u32[]{:S(2)}) %collective-permute-start.25) | collective-permute-done | bytes 1048608 | tf_op jit(solution)/shard_map/ppermute | solution.py:595
  216.5 1.6 fill_other_half.1
  (67 shorter events, 9.2 us)
Async XLA Ops:
  1.4 25.3 %copy-start = (bf16[256,2048]{1,0:T(8,128)(2,1)}, bf16[256,2048]{1,0:T(8,128)(2,1)S(1)}, u32[]{:S(2)}) copy-start(bf16[256,2048]{1,0:T(8,128)(2,1)S(1)} %take_rows.2.refs_0_) | copy-start | bytes 3145732
  1.4 25.3 %collective-permute-start.1 = (bf16[256,2048]{1,0:T(8,128)(2,1)S(1)}, bf16[256,2048]{1,0:T(8,128)(2,1)}, u32[]{:S(2)}, u32[]{:S(2)}) collective-permute-start(bf16[256,2048]{1,0:T(8,128)(2,1)S(1)} %take_rows.2.refs_0_), channel_id=1, source_target_pairs={{0,1},{1,0},{2,3},{3,2},{4,5},{5,4},{6,7},{7,6},{8,9},{9,8},{10,11... | collective-permute-start | bytes 3145736 | tf_op jit(solution)/shard_map/ppermute | solution.py:610
  2.7 28.4 %collective-permute-start = (bf16[512,2048]{1,0:T(8,128)(2,1)S(1)}, bf16[512,2048]{1,0:T(8,128)(2,1)}, u32[]{:S(2)}, u32[]{:S(2)}) collective-permute-start(bf16[512,2048]{1,0:T(8,128)(2,1)S(1)} %bitcast.18), channel_id=1, source_target_pairs={{0,2},{2,0},{4,6},{6,4},{8,10},{10,8},{12,14},{14,12},{1,3},{3,1},... | collective-permute-start | bytes 6291464 | tf_op jit(solution)/shard_map/ppermute | solution.py:595
  26.8 4.3 %collective-permute-start.2 = (bf16[256,2048]{1,0:T(8,128)(2,1)}, bf16[256,2048]{1,0:T(8,128)(2,1)S(1)}, u32[]{:S(2)}, u32[]{:S(2)}) collective-permute-start(bf16[256,2048]{1,0:T(8,128)(2,1)} %after_all.3.oth), channel_id=1, source_target_pairs={{0,2},{2,0},{4,6},{6,4},{8,10},{10,8},{12,14},{14,12},{1,3},{3,1},... | collective-permute-start | bytes 3145736 | tf_op jit(solution)/shard_map/ppermute | solution.py:595
  29.3 25.8 %collective-permute-start.3 = (bf16[256,2048]{1,0:T(8,128)(2,1)}, bf16[256,2048]{1,0:T(8,128)(2,1)}, u32[]{:S(2)}, u32[]{:S(2)}) collective-permute-start(bf16[256,2048]{1,0:T(8,128)(2,1)} %take_rows.3), channel_id=1, source_target_pairs={{0,1},{1,0},{2,3},{3,2},{4,5},{5,4},{6,7},{7,6},{8,9},{9,8},{10,11... | collective-permute-start | bytes 3145736 | tf_op jit(solution)/shard_map/ppermute | solution.py:610
  55.0 2.9 %collective-permute-start.4 = (bf16[256,2048]{1,0:T(8,128)(2,1)}, bf16[256,2048]{1,0:T(8,128)(2,1)S(1)}, u32[]{:S(2)}, u32[]{:S(2)}) collective-permute-start(bf16[256,2048]{1,0:T(8,128)(2,1)} %after_all.4.oth), channel_id=1, source_target_pairs={{0,2},{2,0},{4,6},{6,4},{8,10},{10,8},{12,14},{14,12},{1,3},{3,1},... | collective-permute-start | bytes 3145736 | tf_op jit(solution)/shard_map/ppermute | solution.py:595
  55.3 30.6 %collective-permute-start.21 = (bf16[2,256,768]{2,1,0:T(8,128)(2,1)}, bf16[2,256,768]{2,1,0:T(8,128)(2,1)}, u32[]{:S(2)}, u32[]{:S(2)}) collective-permute-start(bf16[2,256,768]{2,1,0:T(8,128)(2,1)} %get-tuple-element.29), channel_id=1, source_target_pairs={{0,2},{2,0},{4,6},{6,4},{8,10},{10,8},{12,14},{14,12},{1,3},{3,1},... | collective-permute-start | bytes 2359304 | tf_op jit(solution)/shard_map/ppermute | solution.py:595
  55.5 18.6 %collective-permute-start.5 = (bf16[528,256]{1,0:T(8,128)(2,1)}, bf16[528,256]{1,0:T(8,128)(2,1)}, u32[]{:S(2)}, u32[]{:S(2)}) collective-permute-start(bf16[528,256]{1,0:T(8,128)(2,1)} %get-tuple-element.25.refs_4_), channel_id=1, source_target_pairs={{0,16},{1,17},{2,18},{3,19},{4,20},{5,21},{6,22},{7,23},{8,24},{9,... | collective-permute-start | bytes 811016 | tf_op jit(solution)/shard_map/ppermute | solution.py:623
  58.9 15.3 %copy-start.12 = (bf16[528,256]{1,0:T(8,128)(2,1)S(1)}, bf16[528,256]{1,0:T(8,128)(2,1)}, u32[]{:S(2)}) copy-start(bf16[528,256]{1,0:T(8,128)(2,1)} %get-tuple-element.24.refs_3_) | copy-start | bytes 811012
  72.8 17.5 %copy-start.3 = (s32[4]{0:T(128)S(1)}, s32[4]{0:T(128)}, u32[]{:S(2)}) copy-start(s32[4]{0:T(128)} %pad_add_fusion.ids) | copy-start | bytes 52
  72.8 17.5 %copy-start.6 = (s32[128]{0:T(128)S(1)}, s32[128]{0:T(128)}, u32[]{:S(2)}) copy-start(s32[128]{0:T(128)} %lens.7) | copy-start | bytes 1540
  72.8 17.5 %copy-start.8 = (s32[128]{0:T(128)S(1)}, s32[128]{0:T(128)}, u32[]{:S(2)}) copy-start(s32[128]{0:T(128)} %receive.7) | copy-start | bytes 1540
  72.8 10.0 %collective-permute-start.13 = (bf16[528,256]{1,0:T(8,128)(2,1)}, bf16[528,256]{1,0:T(8,128)(2,1)S(1)}, u32[]{:S(2)}, u32[]{:S(2)}) collective-permute-start(bf16[528,256]{1,0:T(8,128)(2,1)} %get-tuple-element.27.refs_6_), channel_id=1, source_target_pairs={{0,16},{1,17},{2,18},{3,19},{4,20},{5,21},{6,22},{7,23},{8,24},{9,... | collective-permute-start | bytes 811016 | tf_op jit(solution)/shard_map/ppermute | solution.py:629
  75.2 11.9 %collective-permute-start.6 = (bf16[528,256]{1,0:T(8,128)(2,1)S(1)}, bf16[528,256]{1,0:T(8,128)(2,1)}, u32[]{:S(2)}, u32[]{:S(2)}) collective-permute-start(bf16[528,256]{1,0:T(8,128)(2,1)S(1)} %broadcast_select_fusion.1.refs_7_), channel_id=1, source_target_pairs={{0,4},{2,6},{4,8},{6,10},{8,12},{10,14},{12,28},{14,30},{28,24},{3... | collective-permute-start | bytes 811016 | tf_op jit(solution)/shard_map/ppermute | solution.py:600
  76.4 12.2 %collective-permute-start.10 = (bf16[528,256]{1,0:T(8,128)(2,1)S(1)}, bf16[528,256]{1,0:T(8,128)(2,1)}, u32[]{:S(2)}, u32[]{:S(2)}) collective-permute-start(bf16[528,256]{1,0:T(8,128)(2,1)S(1)} %broadcast_select_fusion.1.refs_7_), channel_id=1, source_target_pairs={{0,16},{2,18},{4,0},{6,2},{8,4},{10,6},{12,8},{14,10},{28,12},{30,... | collective-permute-start | bytes 811016 | tf_op jit(solution)/shard_map/ppermute | solution.py:602
  83.5 6.6 %collective-permute-start.14 = (bf16[528,256]{1,0:T(8,128)(2,1)}, bf16[528,256]{1,0:T(8,128)(2,1)}, u32[]{:S(2)}, u32[]{:S(2)}) collective-permute-start(bf16[528,256]{1,0:T(8,128)(2,1)} %broadcast_select_fusion.refs_15_), channel_id=1, source_target_pairs={{0,4},{2,6},{4,8},{6,10},{8,12},{10,14},{12,28},{14,30},{28,24},{3... | collective-permute-start | bytes 811016 | tf_op jit(solution)/shard_map/ppermute | solution.py:600
  83.8 21.9 %collective-permute-start.23 = (bf16[2,256,768]{2,1,0:T(8,128)(2,1)}, bf16[2,256,768]{2,1,0:T(8,128)(2,1)}, u32[]{:S(2)}, u32[]{:S(2)}) collective-permute-start(bf16[2,256,768]{2,1,0:T(8,128)(2,1)} %get-tuple-element.30), channel_id=1, source_target_pairs={{0,2},{2,0},{4,6},{6,4},{8,10},{10,8},{12,14},{14,12},{1,3},{3,1},... | collective-permute-start | bytes 2359304 | tf_op jit(solution)/shard_map/ppermute | solution.py:595
  85.9 13.1 %collective-permute-start.18 = (bf16[528,256]{1,0:T(8,128)(2,1)}, bf16[528,256]{1,0:T(8,128)(2,1)}, u32[]{:S(2)}, u32[]{:S(2)}) collective-permute-start(bf16[528,256]{1,0:T(8,128)(2,1)} %broadcast_select_fusion.refs_15_), channel_id=1, source_target_pairs={{0,16},{2,18},{4,0},{6,2},{8,4},{10,6},{12,8},{14,10},{28,12},{30,... | collective-permute-start | bytes 811016 | tf_op jit(solution)/shard_map/ppermute | solution.py:602
  87.0 17.2 %collective-permute-start.7 = (bf16[528,256]{1,0:T(8,128)(2,1)}, bf16[528,256]{1,0:T(8,128)(2,1)}, u32[]{:S(2)}, u32[]{:S(2)}) collective-permute-start(bf16[528,256]{1,0:T(8,128)(2,1)} %collective-permute-done.6.refs_8_), channel_id=1, source_target_pairs={{0,4},{2,6},{4,8},{6,10},{8,12},{10,14},{12,28},{14,30},{28,24},{3... | collective-permute-start | bytes 811016 | tf_op jit(solution)/shard_map/ppermute | solution.py:600
  88.6 16.9 %collective-permute-start.11 = (bf16[528,256]{1,0:T(8,128)(2,1)}, bf16[528,256]{1,0:T(8,128)(2,1)}, u32[]{:S(2)}, u32[]{:S(2)}) collective-permute-start(bf16[528,256]{1,0:T(8,128)(2,1)} %collective-permute-done.10.refs_14_), channel_id=1, source_target_pairs={{0,16},{2,18},{4,0},{6,2},{8,4},{10,6},{12,8},{14,10},{28,12},{30,... | collective-permute-start | bytes 811016 | tf_op jit(solution)/shard_map/ppermute | solution.py:602
  90.1 16.8 %collective-permute-start.15 = (bf16[528,256]{1,0:T(8,128)(2,1)}, bf16[528,256]{1,0:T(8,128)(2,1)}, u32[]{:S(2)}, u32[]{:S(2)}) collective-permute-start(bf16[528,256]{1,0:T(8,128)(2,1)} %collective-permute-done.14.refs_16_), channel_id=1, source_target_pairs={{0,4},{2,6},{4,8},{6,10},{8,12},{10,14},{12,28},{14,30},{28,24},{3... | collective-permute-start | bytes 811016 | tf_op jit(solution)/shard_map/ppermute | solution.py:600
  99.0 29.7 %collective-permute-start.22 = (f32[2,256,640]{2,1,0:T(8,128)}, f32[2,256,640]{2,1,0:T(8,128)}, u32[]{:S(2)}, u32[]{:S(2)}) collective-permute-start(f32[2,256,640]{2,1,0:T(8,128)} %cache_attention.5.refs_1_), channel_id=1, source_target_pairs={{0,2},{2,0},{4,6},{6,4},{8,10},{10,8},{12,14},{14,12},{1,3},{3,1},... | collective-permute-start | bytes 3932168 | tf_op jit(solution)/shard_map/ppermute | solution.py:595
  104.2 11.7 %collective-permute-start.19 = (bf16[528,256]{1,0:T(8,128)(2,1)}, bf16[528,256]{1,0:T(8,128)(2,1)}, u32[]{:S(2)}, u32[]{:S(2)}) collective-permute-start(bf16[528,256]{1,0:T(8,128)(2,1)} %collective-permute-done.18.refs_22_), channel_id=1, source_target_pairs={{0,16},{2,18},{4,0},{6,2},{8,4},{10,6},{12,8},{14,10},{28,12},{30,... | collective-permute-start | bytes 811016 | tf_op jit(solution)/shard_map/ppermute | solution.py:602
  105.5 11.6 %collective-permute-start.8 = (bf16[528,256]{1,0:T(8,128)(2,1)}, bf16[528,256]{1,0:T(8,128)(2,1)}, u32[]{:S(2)}, u32[]{:S(2)}) collective-permute-start(bf16[528,256]{1,0:T(8,128)(2,1)} %collective-permute-done.7.refs_9_), channel_id=1, source_target_pairs={{0,4},{2,6},{4,8},{6,10},{8,12},{10,14},{12,28},{14,30},{28,24},{3... | collective-permute-start | bytes 811016 | tf_op jit(solution)/shard_map/ppermute | solution.py:600
  105.7 12.7 %collective-permute-start.12 = (bf16[528,256]{1,0:T(8,128)(2,1)}, bf16[528,256]{1,0:T(8,128)(2,1)}, u32[]{:S(2)}, u32[]{:S(2)}) collective-permute-start(bf16[528,256]{1,0:T(8,128)(2,1)} %collective-permute-done.11.refs_13_), channel_id=1, source_target_pairs={{0,16},{2,18},{4,0},{6,2},{8,4},{10,6},{12,8},{14,10},{28,12},{30,... | collective-permute-start | bytes 811016 | tf_op jit(solution)/shard_map/ppermute | solution.py:602
  107.0 12.4 %collective-permute-start.16 = (bf16[528,256]{1,0:T(8,128)(2,1)}, bf16[528,256]{1,0:T(8,128)(2,1)}, u32[]{:S(2)}, u32[]{:S(2)}) collective-permute-start(bf16[528,256]{1,0:T(8,128)(2,1)} %collective-permute-done.15.refs_17_), channel_id=1, source_target_pairs={{0,4},{2,6},{4,8},{6,10},{8,12},{10,14},{12,28},{14,30},{28,24},{3... | collective-permute-start | bytes 811016 | tf_op jit(solution)/shard_map/ppermute | solution.py:600
  115.9 16.3 %collective-permute-start.24 = (f32[2,256,640]{2,1,0:T(8,128)}, f32[2,256,640]{2,1,0:T(8,128)}, u32[]{:S(2)}, u32[]{:S(2)}) collective-permute-start(f32[2,256,640]{2,1,0:T(8,128)} %cache_attention.6.refs_2_), channel_id=1, source_target_pairs={{0,2},{2,0},{4,6},{6,4},{8,10},{10,8},{12,14},{14,12},{1,3},{3,1},... | collective-permute-start | bytes 3932168 | tf_op jit(solution)/shard_map/ppermute | solution.py:595
  117.1 11.6 %collective-permute-start.20 = (bf16[528,256]{1,0:T(8,128)(2,1)}, bf16[528,256]{1,0:T(8,128)(2,1)}, u32[]{:S(2)}, u32[]{:S(2)}) collective-permute-start(bf16[528,256]{1,0:T(8,128)(2,1)} %collective-permute-done.19.refs_21_), channel_id=1, source_target_pairs={{0,16},{2,18},{4,0},{6,2},{8,4},{10,6},{12,8},{14,10},{28,12},{30,... | collective-permute-start | bytes 811016 | tf_op jit(solution)/shard_map/ppermute | solution.py:602
  118.4 10.3 %collective-permute-start.9 = (bf16[528,256]{1,0:T(8,128)(2,1)}, bf16[528,256]{1,0:T(8,128)(2,1)}, u32[]{:S(2)}, u32[]{:S(2)}) collective-permute-start(bf16[528,256]{1,0:T(8,128)(2,1)} %collective-permute-done.8.refs_10_), channel_id=1, source_target_pairs={{0,4},{2,6},{4,8},{6,10},{8,12},{10,14},{12,28},{14,30},{28,24},{3... | collective-permute-start | bytes 811016 | tf_op jit(solution)/shard_map/ppermute | solution.py:600
  119.3 12.8 %collective-permute-start.17 = (bf16[528,256]{1,0:T(8,128)(2,1)}, bf16[528,256]{1,0:T(8,128)(2,1)}, u32[]{:S(2)}, u32[]{:S(2)}) collective-permute-start(bf16[528,256]{1,0:T(8,128)(2,1)} %collective-permute-done.16.refs_18_), channel_id=1, source_target_pairs={{0,4},{2,6},{4,8},{6,10},{8,12},{10,14},{12,28},{14,30},{28,24},{3... | collective-permute-start | bytes 811016 | tf_op jit(solution)/shard_map/ppermute | solution.py:600
  132.1 84.3 %copy-start.4 = (s32[4]{0:T(128)S(1)}, s32[4]{0:T(128)}, u32[]{:S(2)}) copy-start(s32[4]{0:T(128)} %pad_add_fusion.ids) | copy-start | bytes 52
  212.4 4.1 %collective-permute-start.25 = (bf16[512,1024]{1,0:T(8,128)(2,1)}, bf16[512,1024]{1,0:T(8,128)(2,1)S(1)}, u32[]{:S(2)}, u32[]{:S(2)}) collective-permute-start(bf16[512,1024]{1,0:T(8,128)(2,1)} %get-tuple-element.32), channel_id=1, source_target_pairs={{0,2},{2,0},{4,6},{6,4},{8,10},{10,8},{12,14},{14,12},{1,3},{3,1},... | collective-permute-start | bytes 3145736 | tf_op jit(solution)/shard_map/ppermute | solution.py:595
  (9 other events, 52.2 us)
